TPU v7x, 32 devices: a whole 2x2x4 slice. The times are simulated.
32 devices in a mesh: fsdp: 32 (over z, y, x, core).
Axes of the slice: x: 2, y: 2, z: 4, core: 2. Of those that a mesh axis runs over, the one named last changes fastest.
Arguments:
- layer_in: bfloat16 [64, 416, 768], P('fsdp'), may hold values from -24 to 24
- pair_ids: int32 [64, 416], P('fsdp'), may hold values from 0 to 2, as said below
- pair_lengths: int32 [64, 3, 2], P('fsdp'), may hold values from 1 to 273, as said below
- attn_shard: bfloat16 [2363392], P('fsdp'), may hold values from -2 to 2
- ffn_shard: bfloat16 [4726784], P('fsdp'), may hold values from -2 to 2
- out_grad: bfloat16 [64, 416, 768], P('fsdp'), may hold values from -8 to 8
Outputs:
- layer_out: bfloat16 [64, 416, 768], P('fsdp')
- in_grad: float32 [64, 416, 768], P('fsdp')
- attn_grad: float32 [2363392], P('fsdp')
- ffn_grad: float32 [4726784], P('fsdp')
- out_bias_grad: float32 [768], replicated
Inputs may be any that keep to these rules, and one draw needn't show every extreme that they name: `pair_ids`: ids never decrease along a row, and every id of 0 to 2 occupies a run of slots in every row. `pair_lengths`: [.., 0] counts text slots and [.., 1] region slots; their sum is at most the pair's run of slots, and the live slots are the first ones of the run.
All inputs are finite; a program needn't handle non-finite values.
Results may differ from a plain program's by a relative error of at most 0.014.
The roundings to bfloat16 on the way count: a program that leaves them out, or rounds other values in their place, can miss the bound.
Values may be sent and summed in bfloat16 or wider, within the bound.
A program may use at most 192 MiB of HBM per device.

v0:
```python
import jax
import jax.numpy as jnp
from jax import lax
from jax.sharding import PartitionSpec as P

D = 768
HEADS = 12
HEAD_DIM = 64
FF = 3072
SLOTS = 416
PAIRS = 3


NORM_EPS = 1e-12


def unpack_attention(flattened):
    offset = 3 * D * D
    weight_joint = flattened[:offset].reshape(D, 3 * D)
    weight_out = flattened[offset : offset + D * D].reshape(D, D)
    offset = offset + D * D
    vectors = flattened[offset : offset + 5 * D].reshape(5, D)
    return (weight_joint, weight_out, vectors[0], vectors[1], vectors[2], vectors[3], vectors[4])


def unpack_feedforward(flattened):
    offset = D * FF
    weight_in = flattened[:offset].reshape(D, FF)
    bias_in = flattened[offset : offset + FF]
    offset = offset + FF
    weight_back = flattened[offset : offset + FF * D].reshape(FF, D)
    offset = offset + FF * D
    vectors = flattened[offset : offset + 3 * D].reshape(3, D)
    return (weight_in, bias_in, weight_back, vectors[0], vectors[1], vectors[2])


def layer_norm(values, gain_vec, shift_vec):
    row_mean = jnp.mean(values, axis=-1, keepdims=True)
    centred = values - row_mean
    row_var = jnp.mean(centred * centred, axis=-1, keepdims=True)
    return centred * lax.rsqrt(row_var + NORM_EPS) * gain_vec + shift_vec


def exact_gelu(values):
    return jax.nn.gelu(values, approximate=False)


def key_mask(pair_ids, pair_lengths):
    labels = jnp.arange(PAIRS, dtype=jnp.int32)
    member = pair_ids[:, :, None] == labels[None, None, :]
    starts = jnp.sum((pair_ids[:, :, None] < labels[None, None, :]).astype(jnp.int32), axis=1)
    live_len = pair_lengths[:, :, 0] + pair_lengths[:, :, 1]
    slot_start = jnp.sum(jnp.where(member, starts[:, None, :], 0), axis=-1)
    slot_len = jnp.sum(jnp.where(member, live_len[:, None, :], 0), axis=-1)
    places = jnp.arange(pair_ids.shape[1], dtype=jnp.int32)[None, :]
    is_live = places - slot_start < slot_len
    return (pair_ids[:, :, None] == pair_ids[:, None, :]) & is_live[:, None, :]


def contract_rows(one_side, other_side):
    return lax.dot_general(
        one_side, other_side, (((0,), (0,)), ((), ())), preferred_element_type=jnp.float32
    )


def contract_cols(one_side, other_side):
    return lax.dot_general(
        one_side, other_side, (((1,), (1,)), ((), ())), preferred_element_type=jnp.float32
    )


def attend_forward(queries, key_rows, value_rows, key_ok, score_scale):

    def head_block(block_index):
        head_start = block_index * 4
        query_b = lax.dynamic_slice_in_dim(queries, head_start, 4, 2)
        key_b = lax.dynamic_slice_in_dim(key_rows, head_start, 4, 2)
        value_b = lax.dynamic_slice_in_dim(value_rows, head_start, 4, 2)
        scores = (
            jnp.einsum("rqhd,rkhd->rhqk", query_b, key_b, preferred_element_type=jnp.float32)
            * score_scale
        )
        scores = jnp.where(key_ok[:, None], scores, -1e30)
        row_max = jnp.max(scores, axis=-1, keepdims=True)
        raised = jnp.exp(scores - row_max)
        totals = jnp.sum(raised, axis=-1, keepdims=True)
        shares = (raised / totals).astype(jnp.bfloat16)
        context = jnp.einsum("rhqk,rkhd->rqhd", shares, value_b, preferred_element_type=jnp.float32)
        return (context, row_max + jnp.log(totals))

    return lax.map(head_block, jnp.arange(HEADS // 4))


def attend_backward(queries, key_rows, value_rows, grad_context, log_totals, key_ok, score_scale):

    def head_block(operands):
        block_index, log_total = operands
        head_start = block_index * 4
        query_b = lax.dynamic_slice_in_dim(queries, head_start, 4, 2)
        key_b = lax.dynamic_slice_in_dim(key_rows, head_start, 4, 2)
        value_b = lax.dynamic_slice_in_dim(value_rows, head_start, 4, 2)
        grad_block = lax.dynamic_slice_in_dim(grad_context, head_start, 4, 2)
        scores = (
            jnp.einsum("rqhd,rkhd->rhqk", query_b, key_b, preferred_element_type=jnp.float32)
            * score_scale
        )
        shares = jnp.where(key_ok[:, None], jnp.exp(scores - log_total), 0.0)
        grad_shares = jnp.einsum(
            "rqhd,rkhd->rhqk", grad_block, value_b, preferred_element_type=jnp.float32
        )
        inner_sum = jnp.sum(shares * grad_shares, axis=-1, keepdims=True)
        grad_scores = (shares * (grad_shares - inner_sum)).astype(jnp.bfloat16)
        grad_query = (
            jnp.einsum("rhqk,rkhd->rqhd", grad_scores, key_b, preferred_element_type=jnp.float32)
            * score_scale
        )
        grad_key = (
            jnp.einsum("rhqk,rqhd->rkhd", grad_scores, query_b, preferred_element_type=jnp.float32)
            * score_scale
        )
        grad_value = jnp.einsum(
            "rhqk,rqhd->rkhd",
            shares.astype(jnp.bfloat16),
            grad_block,
            preferred_element_type=jnp.float32,
        )
        return (grad_query, grad_key, grad_value)

    gradients = lax.map(head_block, (jnp.arange(HEADS // 4), log_totals))
    return [jnp.moveaxis(piece, 0, 2).reshape(-1, D) for piece in gradients]


def body(layer_in, pair_ids, pair_lengths, attn_shard, ffn_shard, out_grad):
    row_count = layer_in.shape[0]
    tokens = row_count * SLOTS
    score_scale = HEAD_DIM ** (-0.5)
    key_ok = key_mask(pair_ids, pair_lengths)
    att_whole = lax.all_gather(attn_shard, "fsdp", axis=0, tiled=True)
    weight_joint, weight_out, bias_query, bias_value, bias_out, gain_first, shift_first = (
        unpack_attention(att_whole)
    )
    inputs = layer_in.reshape(tokens, D)
    bias_joint = jnp.concatenate([bias_query, jnp.zeros_like(bias_query), bias_value]).astype(
        jnp.float32
    )
    projected = (
        jnp.dot(inputs, weight_joint, preferred_element_type=jnp.float32) + bias_joint
    ).astype(jnp.bfloat16)
    projected = projected.reshape(row_count, SLOTS, 3, HEADS, HEAD_DIM)
    queries = projected[:, :, 0]
    key_rows = projected[:, :, 1]
    value_rows = projected[:, :, 2]
    contexts, log_totals = attend_forward(queries, key_rows, value_rows, key_ok, score_scale)
    context = jnp.moveaxis(contexts, 0, 2).reshape(tokens, D).astype(jnp.bfloat16)
    attn_out = jnp.dot(context, weight_out, preferred_element_type=jnp.float32) + bias_out.astype(
        jnp.float32
    )
    norm_first, first_pull = jax.vjp(
        layer_norm,
        inputs.astype(jnp.float32) + attn_out,
        gain_first.astype(jnp.float32),
        shift_first.astype(jnp.float32),
    )
    norm_first_b = norm_first.astype(jnp.bfloat16)
    feed_whole = lax.all_gather(ffn_shard, "fsdp", axis=0, tiled=True)
    weight_in, bias_in, weight_back, bias_back, gain_second, shift_second = unpack_feedforward(
        feed_whole
    )
    hidden = jnp.dot(norm_first_b, weight_in, preferred_element_type=jnp.float32) + bias_in.astype(
        jnp.float32
    )
    active, gelu_pull = jax.vjp(exact_gelu, hidden)
    active_b = active.astype(jnp.bfloat16)
    ffn_out = jnp.dot(active_b, weight_back, preferred_element_type=jnp.float32) + bias_back.astype(
        jnp.float32
    )
    result, second_pull = jax.vjp(
        layer_norm,
        norm_first + ffn_out,
        gain_second.astype(jnp.float32),
        shift_second.astype(jnp.float32),
    )
    layer_out = result.astype(jnp.bfloat16).reshape(row_count, SLOTS, D)
    feed_back = lax.all_gather(ffn_shard, "fsdp", axis=0, tiled=True)
    weight_in, bias_in, weight_back, bias_back, gain_second, shift_second = unpack_feedforward(
        feed_back
    )
    cotangent = out_grad.reshape(tokens, D).astype(jnp.float32)
    grad_sum_second, grad_gain_second, grad_shift_second = second_pull(cotangent)
    grad_ffn = grad_sum_second.astype(jnp.bfloat16)
    grad_bias_back = jnp.sum(grad_ffn.astype(jnp.float32), axis=0)
    grad_weight_back = contract_rows(active_b, grad_ffn)
    (grad_hidden,) = gelu_pull(contract_cols(grad_ffn, weight_back))
    grad_hidden = grad_hidden.astype(jnp.bfloat16)
    grad_bias_in = jnp.sum(grad_hidden.astype(jnp.float32), axis=0)
    grad_weight_in = contract_rows(norm_first_b, grad_hidden)
    grad_norm_first = grad_sum_second + contract_cols(grad_hidden, weight_in)
    grad_sum_first, grad_gain_first, grad_shift_first = first_pull(grad_norm_first)
    feed_pad = feed_back.shape[0] - (2 * D * FF + FF + 3 * D)
    feed_full = jnp.concatenate(
        [
            grad_weight_in.reshape(-1),
            grad_bias_in,
            grad_weight_back.reshape(-1),
            grad_bias_back,
            grad_gain_second,
            grad_shift_second,
            jnp.zeros((feed_pad,), jnp.float32),
        ]
    )
    ffn_grad = lax.psum_scatter(feed_full, "fsdp", scatter_dimension=0, tiled=True)
    att_back = lax.all_gather(attn_shard, "fsdp", axis=0, tiled=True)
    weight_joint, weight_out, bias_query, bias_value, bias_out, gain_first, shift_first = (
        unpack_attention(att_back)
    )
    grad_attn = grad_sum_first.astype(jnp.bfloat16)
    grad_bias_out = jnp.sum(grad_attn.astype(jnp.float32), axis=0)
    out_bias_grad = lax.psum(grad_bias_out, "fsdp")
    grad_weight_out = contract_rows(context, grad_attn)
    grad_context = (
        contract_cols(grad_attn, weight_out)
        .astype(jnp.bfloat16)
        .reshape(row_count, SLOTS, HEADS, HEAD_DIM)
    )
    grad_query, grad_key, grad_value = attend_backward(
        queries, key_rows, value_rows, grad_context, log_totals, key_ok, score_scale
    )
    grad_projected = jnp.concatenate([grad_query, grad_key, grad_value], axis=-1).astype(
        jnp.bfloat16
    )
    column_sums = jnp.sum(grad_projected.astype(jnp.float32), axis=0)
    grad_weight_joint = contract_rows(inputs, grad_projected)
    in_grad = grad_sum_first + contract_cols(grad_projected, weight_joint)
    att_pad = att_back.shape[0] - (4 * D * D + 5 * D)
    attn_full = jnp.concatenate(
        [
            grad_weight_joint.reshape(-1),
            grad_weight_out.reshape(-1),
            column_sums[:D],
            column_sums[2 * D :],
            grad_bias_out,
            grad_gain_first,
            grad_shift_first,
            jnp.zeros((att_pad,), jnp.float32),
        ]
    )
    attn_grad = lax.psum_scatter(attn_full, "fsdp", scatter_dimension=0, tiled=True)
    return (layer_out, in_grad.reshape(row_count, SLOTS, D), attn_grad, ffn_grad, out_bias_grad)


def solution(mesh):
    placed = (
        P("fsdp", None, None),
        P("fsdp", None),
        P("fsdp", None, None),
        P("fsdp"),
        P("fsdp"),
        P("fsdp", None, None),
    )
    return jax.shard_map(
        body,
        mesh=mesh,
        in_specs=placed,
        out_specs=(P("fsdp", None, None), P("fsdp", None, None), P("fsdp"), P("fsdp"), P()),
        check_vma=False,
    )
```

profile of v0, /device:TPU:1, one launch (start us, length us, event | category | flops | bytes accessed | tf_op | source)
XLA Modules:
  0.0 1187.5 jit_solution(14004726989603011789)
XLA Ops:
  18.2 78.0 %all-gather.5.cloned.1.call-done = bf16[32,1,73856]{2,1,0:T(2,128)(2,1)} async-done(((bf16[1,1,73856]{2,1,0:T(2,128)(2,1)}), bf16[32,1,73856]{2,1,0:T(2,128)(2,1)}) %all-gather.5.cloned.1.call-update) | async-done | bytes 4726800 | tf_op jit(solution)/shard_map/all_gather | solution.py:138
  96.1 101.1 %reduce.1 = bf16[32,73856]{1,0:T(8,128)(2,1)} reduce(bf16[32,1,73856]{2,1,0:T(2,128)(2,1)} %all-gather.5.cloned.1.call-done, bf16[]{:T(256)} %constant.139), dimensions={1}, to_apply=%all-gather.reduce_sub_computation | reduce | bytes 9453570 | tf_op jit(solution)/shard_map/all_gather | solution.py:138
  197.2 9.4 reshape.259
  214.9 7.8 add_convert_fusion.1
  229.0 14.8 %reshape.243 = bf16[2,416,3,12,64]{1,0,4,3,2:T(2,128)(2,1)} reshape(bf16[832,2304]{0,1:T(8,128)(2,1)} %copy.59) | data formatting | bytes 7667712 | tf_op jit(solution)/shard_map/reshape | solution.py:149
  254.3 30.4 %while.28 = (s32[]{:T(128)}, bf16[3,2,416,4,64]{2,4,3,1,0:T(8,128)(2,1)}, f32[3,2,4,416,1]{3,2,1,4,0:T(4,128)}, s32[3]{0:T(128)S(1)}, bf16[2,416,12,64]{1,3,2,0:...) while((s32[]{:T(128)}, ...), condition=%wide.region_6.7_spmd.clone, body=%wide.region_3.6_spmd.clone.sunk | while | flops 371720960 | bytes 32401732 | solution.py:91
  300.3 153.4 %reduce.2 = bf16[32,147712]{1,0:T(8,128)(2,1)} reduce(bf16[32,1,147712]{2,1,0:T(2,128)(2,1)} %all-gather.7.cloned.1.call-done, bf16[]{:T(256)} %constant.139), dimensions={1}, to_apply=%all-gather.1.reduce_sub_computation | reduce | bytes 18907138 | tf_op jit(solution)/shard_map/all_gather | solution.py:165
  453.7 17.3 %reshape.261 = bf16[4726784]{0:T(1024)(128)(2,1)} reshape(bf16[32,147712]{1,0:T(8,128)(2,1)} %reduce.2) | data formatting | bytes 18907136
  472.4 8.3 fusion.63
  480.7 8.4 reshape.245
  489.1 9.2 reshape.246
  498.4 29.9 %multiply_convert_fusion.1 = (bf16[832,3072]{1,0:T(8,128)(2,1)S(1)}, f32[832,3072]{1,0:T(8,128)}, f32[832,3072]{1,0:T(8,128)}) fusion(f32[3072]{0:T(1024)S(1)} %slice_convert_fusion, bf16[768,3072]{1,0:T(8,128)(2,1)} %reshape.245, f32[832,768]{1,0:T(8,128)S(1)} %get-tuple-element.318, f32[768]{0:T(1024)S(1)} %get-tuple-element.308, ...), kind=kOutput, calls=%fused_computation.56 | convolution fusion | flops 4097753088 | bytes 32858624 | tf_op jit(solution)/shard_map/dot_general | solution.py:169
  541.7 13.6 %convert_reduce_fusion = (f32[3072]{0:T(1024)}, bf16[832,3072]{1,0:T(8,128)(2,1)S(1)}) fusion(f32[832,3072]{1,0:T(8,128)} %get-tuple-element.297, f32[832,3072]{1,0:T(8,128)} %get-tuple-element.319, f32[3072]{0:T(1024)S(1)} %slice_convert_fusion, bf16[832,768]{1,0:T(8,128)(2,1)S(1)} %get-tuple-element.289, bf16[3072,768]{1,0:T(8,128)(2,1)} %reshape.246), kind=kOutput, calls=%fused_computation.54 | convolution fusion | flops 3969315840 | bytes 31580160 | tf_op jit(solution)/shard_map/dot_general | solution.py:67
  555.3 9.0 multiply_reduce_fusion.1
  582.9 44.0 %while.29 = (s32[]{:T(128)}, bf16[3,2,416,4,64]{2,4,3,1,0:T(8,128)(2,1)}, bf16[3,2,416,4,64]{2,4,3,1,0:T(8,128)(2,1)}, bf16[3,2,416,4,64]{2,4,3,1,0:T(8,128)(2,1...) while((s32[]{:T(128)}, ...), condition=%wide.region_17.18_spmd.clone, body=%wide.region_15.17_spmd.clone.sunk | while | flops 907928320 | bytes 89615856 | solution.py:129
  649.6 8.1 convolution_bitcast_fusion
  659.4 8.3 convolution_bitcast_fusion.1
  675.5 8.2 copy.73
  683.7 7.9 reshape.253
  718.2 10.8 reshape.256
  729.6 8.4 constant_dynamic-update-slice_fusion.6
  743.2 41.1 %psum.7 = f32[768]{0:T(1024)} all-reduce(f32[768]{0:T(1024)S(1)} %get-tuple-element.292), channel_id=1, replica_groups=mesh['fsdp'=32] {'fsdp'}, use_global_device_ids=true, to_apply=%region_28.29 | all-reduce | flops 768 | bytes 6144 | tf_op jit(solution)/shard_map/psum | solution.py:218
  784.3 8.6 add_add_fusion.4
  792.9 384.0 %all-reduce.5.cloned.1.call-done = (f32[2363392]{0:T(1024)}, f32[4726784]{0:T(1024)}) async-done(((f32[2363392]{0:T(1024)}, f32[4726784]{0:T(1024)}), (f32[2363392]{0:T(1024)}, f32[4726784]{0:T(1024)})) %all-reduce.5.cloned.1.call-update) | async-done | bytes 28360720
  (269 shorter events, 222.8 us)
Async XLA Ops:
  7.2 89.0 %all-gather.5.cloned.1.call-start = ((), (), s32[]{:S(2)}) async-start(), calls=%async_computation | async-start | bytes 9748992 | tf_op jit(solution)/shard_map/all_gather | solution.py:138
  9.0 291.2 %all-gather.7.cloned.1.call-start = ((), (), s32[]{:S(2)}) async-start(), calls=%async_computation.1 | async-start | bytes 19497984 | tf_op jit(solution)/shard_map/all_gather | solution.py:165
  13.5 1163.4 %all-reduce.5.cloned.1.call-start = ((), (), s32[]{:S(2)}) async-start(), calls=%async_computation.2 | async-start | bytes 56721408
  214.9 313.4 %copy-start.31 = (f32[768]{0:T(1024)}, f32[768]{0:T(1024)S(1)}, u32[]{:S(2)}) copy-start(f32[768]{0:T(1024)S(1)} %get-tuple-element.308) | copy-start | bytes 9220
  284.7 11.6 copy-start
  284.7 11.6 copy-start.29
  284.7 9.6 slice-start.1
  299.7 264.6 %copy-start.3 = (f32[832,768]{1,0:T(8,128)}, f32[832,768]{1,0:T(8,128)S(1)}, u32[]{:S(2)}) copy-start(f32[832,768]{1,0:T(8,128)S(1)} %get-tuple-element.318) | copy-start | bytes 7667716
  300.2 153.5 %copy-start.33 = (f32[832]{0:T(1024)}, f32[832]{0:T(1024)S(1)}, u32[]{:S(2)}) copy-start(f32[832]{0:T(1024)S(1)} %multiply_reduce_fusion.5) | copy-start | bytes 9988
  498.4 29.9 %copy-start.22 = (bf16[3072,768]{1,0:T(8,128)(2,1)S(1)}, bf16[3072,768]{1,0:T(8,128)(2,1)}, u32[]{:S(2)}) copy-start(bf16[3072,768]{1,0:T(8,128)(2,1)} %reshape.246) | copy-start | bytes 14155780
  541.7 13.6 %copy-start.26 = (bf16[832,768]{1,0:T(8,128)(2,1)}, bf16[832,768]{1,0:T(8,128)(2,1)S(1)}, u32[]{:S(2)}) copy-start(bf16[832,768]{1,0:T(8,128)(2,1)S(1)} %get-tuple-element.289) | copy-start | bytes 3833860
  541.7 13.6 %copy-start.5 = (f32[832,768]{1,0:T(8,128)S(1)}, f32[832,768]{1,0:T(8,128)}, u32[]{:S(2)}) copy-start(f32[832,768]{1,0:T(8,128)} %get-tuple-element.315) | copy-start | bytes 7667716
  573.8 9.1 copy-start.2
  573.8 9.1 copy-start.24
  573.8 9.1 copy-start.30
  632.2 10.6 copy-start.19
  645.6 12.8 %slice-start.2 = ((s8[5111808]{0:T(1024)(128)(4,1)}), s8[4194304]{0:T(1024)(128)(4,1)S(1)}, s32[]{:S(2)}) async-start(s8[5111808]{0:T(1024)(128)(4,1)} %bitcast.119), calls=%async_computation.5 | async-start | bytes 8388608
  645.6 22.2 %slice-start.4 = ((s8[5111808]{0:T(1024)(128)(4,1)}), s8[4194304]{0:T(1024)(128)(4,1)S(1)}, s32[]{:S(2)}) async-start(s8[5111808]{0:T(1024)(128)(4,1)} %bitcast.131), calls=%async_computation.7 | async-start | bytes 8388608
  649.6 18.2 %slice-start.5 = ((s8[5111808]{0:T(1024)(128)(4,1)}), s8[917504]{0:T(1024)(128)(4,1)S(1)}, s32[]{:S(2)}) async-start(s8[5111808]{0:T(1024)(128)(4,1)} %bitcast.131), calls=%async_computation.8 | async-start | bytes 1835008
  718.2 10.8 copy-start.40
  729.6 9.7 copy-start.36
  729.6 11.0 copy-start.35
  743.2 41.1 %copy-start.9 = (f32[832,768]{1,0:T(8,128)S(1)}, f32[832,768]{1,0:T(8,128)}, u32[]{:S(2)}) copy-start(f32[832,768]{1,0:T(8,128)} %copy-done.8) | copy-start | bytes 7667716
  743.2 41.1 %copy-start.38 = (f32[832]{0:T(1024)S(1)}, f32[832]{0:T(1024)}, u32[]{:S(2)}) copy-start(f32[832]{0:T(1024)} %copy-done.37) | copy-start | bytes 9988
  (46 other events, 148.5 us)
Sparse Core Ops, SparseCore 0:
  11.5 84.5 all-gather.4
  99.7 123.3 all-gather.6
  743.3 433.4 all-reduce.4
where the time goes:
time: 1190 us
  waiting for transfers between devices  462 us (39%)
  other arithmetic  288 us (24%)
  local copies, waits for them, and re-layouts  231 us (19%)
  matrix products  147 us (12%)
  blocking collectives  41.1 us (3%)
  between operations  14.4 us (1%)
    unnamed x4, waiting for transfers between devices  384 us
    all_gather x1, other arithmetic, body(): feed_whole = lax.all_gather(ffn_shard, 'fsdp', axis=0, tiled=True)  153 us
    all_gather x1, other arithmetic, body(): att_whole = lax.all_gather(attn_shard, 'fsdp', axis=0, tiled=True)  101 us
    unnamed x102, local copies, waits for them, and re-layouts  88.3 us
    all_gather x1, waiting for transfers between devices, body(): att_whole = lax.all_gather(attn_shard, 'fsdp', axis=0, tiled=True)  78 us
    psum x1, blocking collectives, body(): out_bias_grad = lax.psum(grad_bias_out, 'fsdp')  41.1 us
    dot_general x4, matrix products, contract_cols(): lax.dot_general(one_side, other_side, (((1,), (1,)), ((), ())), preferred...  32.3 us
    dot_general x1, matrix products, body(): jnp.dot(norm_first_b, weight_in, preferred_element_type=jnp.float32)  29.9 us
  transfers between devices with their start and end apart: 3, of which 2 were waited for; matrix products, arithmetic and copies ran while one was open for 18% of the time, Pallas kernels for 0%

commit v1 on v0

--- a/solution.py
+++ b/solution.py
@@ -1,6 +1,10 @@
+import functools
+
 import jax
 import jax.numpy as jnp
 from jax import lax
+from jax.experimental import pallas as pl
+from jax.experimental.pallas import tpu as pltpu
 from jax.sharding import PartitionSpec as P
 
 D = 768
@@ -9,9 +13,1274 @@
 FF = 3072
 SLOTS = 416
 PAIRS = 3
-
-
+LANES = 128
 NORM_EPS = 1e-12
+F32 = jnp.float32
+BF16 = jnp.bfloat16
+MESH = pl.DeviceIdType.MESH
+VMEM_LIMIT = 62 << 20
+
+
+def dot_nn(a, b):
+    return lax.dot_general(a, b, (((1,), (0,)), ((), ())), preferred_element_type=F32)
+
+
+def dot_nt(a, b):
+    return lax.dot_general(a, b, (((1,), (1,)), ((), ())), preferred_element_type=F32)
+
+
+def dot_tn(a, b):
+    return lax.dot_general(a, b, (((0,), (0,)), ((), ())), preferred_element_type=F32)
+
+
+def row_mean(v):
+    return jnp.sum(v, axis=1, keepdims=True) * (1.0 / D)
+
+
+def col_sum(v):
+    return jnp.sum(v, axis=0, keepdims=True)
+
+
+class Plan:
+    def __init__(self, n, attn_shard_len, ffn_shard_len, row_count):
+        self.n = n
+        self.nz = n // 8
+        self.rows = row_count
+        self.tokens = row_count * SLOTS
+        self.unit_a = attn_shard_len // LANES
+        self.unit_f = ffn_shard_len // LANES
+        self.block_a = 4 * D * D // LANES // n
+        self.block_f = 2 * D * FF // LANES // n
+        self.rows_a = 4 * D // n
+        self.rows_f = 2 * FF // n
+        self.joint_rows = self.rows_a // 3
+        self.joint_src = 3 * n // 4
+        self.in_rows = self.rows_f // 4
+        self.in_src = n // 2
+        self.late_a = 16
+        self.late_f = 48
+        self.half_a = 32
+        self.half_f = 64
+        self.gap = FF // LANES
+        self.at_attn_vec = divmod(4 * D * D // LANES, self.unit_a)
+        self.at_bias_in = divmod(D * FF // LANES, self.unit_f)
+        self.at_ffn_vec = divmod(2 * D * FF // LANES + self.gap, self.unit_f)
+
+    def shift_a(self, me):
+        return me * (self.unit_a - self.block_a)
+
+    def shift_f(self, me):
+        return me * (self.unit_f - self.block_f) - jnp.where(me >= self.in_src, self.gap, 0)
+
+    def fits(self):
+        n = self.n
+        if n < 16 or n & (n - 1) or 4 * D % n or self.rows_a % 48 or self.rows_f % 64:
+            return False
+        last_a = (n - 1) * (self.unit_a - self.block_a)
+        step_f = self.unit_f - self.block_f
+        last_f = max((self.in_src - 1) * step_f, (n - 1) * step_f - self.gap)
+        first_f = self.in_src * step_f - self.gap
+        self.tail_a = -(-(last_a + 1) // 8) * 8
+        self.tail_f = -(-(last_f + 2) // 8) * 8
+        vec_a, vec_f = 5 * D // LANES, 3 * D // LANES
+        return (
+            step_f >= 0
+            and self.unit_a >= self.block_a
+            and first_f >= 0
+            and self.tail_a <= self.block_a
+            and self.tail_f <= self.block_f
+            and self.at_attn_vec[0] == n - 1
+            and self.at_ffn_vec[0] == n - 1
+            and self.at_bias_in[0] == self.in_src - 1
+            and self.unit_a - self.at_attn_vec[1] <= self.tail_a
+            and self.unit_f - self.at_ffn_vec[1] <= self.tail_f
+            and self.at_attn_vec[1] + vec_a <= self.unit_a
+            and self.at_ffn_vec[1] + vec_f <= self.unit_f
+            and self.at_bias_in[1] + self.gap <= self.unit_f
+            and self.at_bias_in[1] == self.block_f - (self.in_src - 1) * step_f
+            and self.rows_a > self.late_a + self.half_a
+            and self.rows_f > self.late_f + self.half_f
+        )
+
+
+class Place:
+    def __init__(self, plan):
+        self.n, self.nz = plan.n, plan.nz
+        me = lax.axis_index("fsdp")
+        self.me = me
+        self.core = lax.rem(me, 2)
+        self.x = lax.rem(me // 2, 2)
+        self.y = lax.rem(me // 4, 2)
+        self.z = me // 8
+        self.sib = me + 1 - 2 * self.core
+        self.xn = me + 2 - 4 * self.x
+        self.yn = me + 4 - 8 * self.y
+
+    def block(self, column, z, other_core=False):
+        x = self.x if column in (0, 2) else 1 - self.x
+        y = self.y if column in (0, 1) else 1 - self.y
+        core = 1 - self.core if other_core else self.core
+        return ((z * 2 + y) * 2 + x) * 2 + core
+
+    def level(self, distance, fn):
+        if distance == 0:
+            fn(self.z)
+            return
+        pl.when(self.z >= distance)(lambda: fn(self.z - distance))
+        pl.when(self.z + distance < self.nz)(lambda: fn(self.z + distance))
+
+    def onward(self, z, fn):
+        pl.when((z <= self.z) & (self.z < self.nz - 1))(lambda: fn(self.me + 8))
+        pl.when((z >= self.z) & (self.z > 0))(lambda: fn(self.me - 8))
+
+    def bits(self):
+        out = []
+        bit = 1
+        while bit < self.n:
+            out.append(self.me + bit - 2 * bit * lax.rem(self.me // bit, 2))
+            bit *= 2
+        return out
+
+    def barrier(self):
+        sem = pltpu.get_barrier_semaphore()
+
+        def tell(partner):
+            pl.semaphore_signal(sem, inc=1, device_id=(partner,), device_id_type=MESH)
+
+        fixed = self.bits()
+        for partner in fixed:
+            tell(partner)
+        z_odd = lax.rem(self.z, 2)
+        far_z = (self.z > 0) & (self.z < self.nz - 1)
+        far = (self.me > 0) & (self.me < self.n - 1)
+        pl.when(far_z)(lambda: tell(self.me - 8 + 16 * z_odd))
+        pl.when(far)(lambda: tell(self.me - 1 + 2 * self.core))
+        pl.semaphore_wait(sem, len(fixed) + far_z.astype(jnp.int32) + far.astype(jnp.int32))
+
+
+class Wire:
+    def __init__(self, send, recv):
+        self.send, self.recv = send, recv
+        self.sent = []
+
+    def copy(self, src, dst, number, partner):
+        return pltpu.make_async_remote_copy(
+            src_ref=src,
+            dst_ref=dst,
+            send_sem=self.send.at[number],
+            recv_sem=self.recv.at[number],
+            device_id=(partner,),
+            device_id_type=MESH,
+        )
+
+
+def add_over_all(place, wire, base, own, held):
+    partners = place.bits()
+
+    def send(s):
+        wire.copy(own.at[s], held.at[s], base + s, partners[s]).start()
+
+    def take(s):
+        wire.copy(own.at[s], held.at[s], base + s, partners[s]).wait()
+        own[s + 1] = own[s] + held[s]
+
+    steps = [lambda: send(0)]
+    for s in range(len(partners)):
+
+        def step(s=s):
+            take(s)
+            if s + 1 < len(partners):
+                send(s + 1)
+
+        steps.append(step)
+    return steps
+
+
+def gather_count(nz):
+    return 17 * nz + 3
+
+
+class Gather:
+    def __init__(self, place, wire, base, ref, rows, late, half):
+        self.p, self.w, self.ref = place, wire, ref
+        nz = place.nz
+        self.early = (0, rows - late)
+        self.late = (rows - late, late)
+        self.first = (0, half)
+        self.second = (half, rows - late - half)
+        self.all = (0, rows)
+        at = [base]
+
+        def take(count):
+            at[0] += count
+            return at[0] - count
+
+        self.line, self.xs, self.ys, self.d1, self.d2 = (take(nz) for _ in range(5))
+        self.sib, self.late_line, self.late_sib = (take(4 * nz) for _ in range(3))
+        self.px, self.py, self.pd = (take(1) for _ in range(3))
+
+    def at(self, column, z, part):
+        return self.ref.at[self.p.block(column, z), pl.ds(*part)]
+
+    def move(self, column, z, part, number, partner):
+        ref = self.at(column, z, part)
+        return self.w.copy(ref, ref, number, partner)
+
+    def send(self, *args):
+        self.move(*args).start()
+
+    def wait(self, column, z, part, number):
+        self.move(column, z, part, number, self.p.sib).wait_recv()
+
+    def to_sib(self, column, z):
+        self.send(column, z, self.early, self.sib + column * self.p.nz + z, self.p.sib)
+
+    def to_sib_late(self, column, z):
+        self.send(column, z, self.late, self.late_sib + column * self.p.nz + z, self.p.sib)
+
+    def spread(self, z):
+        p = self.p
+        p.onward(z, lambda partner: self.send(0, z, self.early, self.line + z, partner))
+        self.send(0, z, self.early, self.xs + z, p.xn)
+        self.send(0, z, self.early, self.ys + z, p.yn)
+        self.to_sib(0, z)
+
+    def spread_late(self, column, z):
+        number = self.late_line + column * self.p.nz + z
+        self.p.onward(z, lambda partner: self.send(column, z, self.late, number, partner))
+        self.to_sib_late(column, z)
+
+    def take_line(self, z):
+        self.wait(0, z, self.early, self.line + z)
+        self.spread(z)
+
+    def take_plane(self, z):
+        self.wait(1, z, self.early, self.xs + z)
+        self.send(1, z, self.first, self.d1 + z, self.p.yn)
+        self.to_sib(1, z)
+        self.wait(2, z, self.early, self.ys + z)
+        self.send(2, z, self.second, self.d2 + z, self.p.xn)
+        self.to_sib(2, z)
+
+    def take_corner(self, z):
+        self.wait(3, z, self.first, self.d1 + z)
+        self.wait(3, z, self.second, self.d2 + z)
+        self.to_sib(3, z)
+
+    def take_late(self, z):
+        for column in range(4):
+            self.wait(column, z, self.late, self.late_line + column * self.p.nz + z)
+            self.spread_late(column, z)
+
+    def begin(self):
+        p = self.p
+        z = p.z
+        self.send(0, z, self.late, self.px, p.xn)
+        self.send(0, z, self.late, self.py, p.yn)
+        self.spread(z)
+
+    def begin_late(self):
+        p = self.p
+        z = p.z
+        self.wait(1, z, self.late, self.px)
+        self.send(1, z, self.late, self.pd, p.yn)
+        self.spread_late(0, z)
+        self.spread_late(1, z)
+        self.wait(2, z, self.late, self.py)
+        self.spread_late(2, z)
+
+    def corner_late(self):
+        self.wait(3, self.p.z, self.late, self.pd)
+        self.spread_late(3, self.p.z)
+
+    def steps(self):
+        p, nz = self.p, self.p.nz
+        out = [self.begin, self.begin_late]
+        for d in range(1, nz + 2):
+            if d < nz:
+                out.append(lambda d=d: p.level(d, self.take_line))
+            if d - 1 < nz:
+                out.append(lambda d=d: p.level(d - 1, self.take_plane))
+            if d == 1:
+                out.append(self.corner_late)
+            if 0 <= d - 2 < nz:
+                out.append(lambda d=d: p.level(d - 2, self.take_corner))
+            if 1 <= d - 1 < nz:
+                out.append(lambda d=d: p.level(d - 1, self.take_late))
+        out.append(self.finish)
+        return out
+
+    def finish(self):
+        p = self.p
+        nz = p.nz
+
+        def one(j, carry):
+            for column in range(4):
+                ref = self.ref.at[p.block(column, j, True)]
+                for part, base in ((self.early, self.sib), (self.late, self.late_sib)):
+                    r = ref.at[pl.ds(*part)]
+                    self.w.copy(r, r, base + column * nz + j, p.sib).wait_recv()
+            return carry
+
+        lax.fori_loop(0, nz, one, 0)
+
+    def drain(self):
+        p = self.p
+        nz = p.nz
+
+        def sent(column, z, part, number):
+            self.move(column, z, part, number, p.sib).wait_send()
+
+        sent(0, p.z, self.late, self.px)
+        sent(0, p.z, self.late, self.py)
+        sent(1, p.z, self.late, self.pd)
+
+        def one(z, carry):
+            p.onward(z, lambda partner: sent(0, z, self.early, self.line + z))
+            sent(0, z, self.early, self.xs + z)
+            sent(0, z, self.early, self.ys + z)
+            sent(1, z, self.first, self.d1 + z)
+            sent(2, z, self.second, self.d2 + z)
+            for column in range(4):
+                number = column * nz + z
+                sent(column, z, self.early, self.sib + number)
+                sent(column, z, self.late, self.late_sib + number)
+                p.onward(z, lambda partner: sent(column, z, self.late, self.late_line + number))
+            return carry
+
+        lax.fori_loop(0, nz, one, 0)
+
+
+class Scatter:
+    def __init__(self, place, wire, base, src, rows, late, half, total, room, loaded):
+        self.p, self.w, self.src, self.total, self.loaded = place, wire, src, total, loaded
+        nz = place.nz
+        self.early = (0, rows - late)
+        self.late = (rows - late, late)
+        self.first = (0, half)
+        self.second = (half, rows - late - half)
+        (self.side, self.in_first, self.in_second, self.in_x, self.in_y, self.in_line, self.in_late,
+         self.in_plane) = room
+        at = [base]
+
+        def take(count):
+            at[0] += count
+            return at[0] - count
+
+        self.sib = take(4 * nz)
+        self.d1, self.d2, self.xs, self.ys = (take(nz) for _ in range(4))
+        self.line = take(nz + 1)
+        self.late_line = take(4 * (nz + 1))
+        self.plane = take(3)
+
+    @staticmethod
+    def rooms(nz, rows, late, half):
+        def room(count, size):
+            return pltpu.VMEM((count, size, D), BF16)
+
+        early = rows - late
+        return [
+            room(4 * nz, rows), room(4 * nz, rows), room(nz, half), room(nz, early - half), room(nz, early),
+            room(nz, early), room(nz + 1, early), room(4 * (nz + 1), late), room(3, late),
+        ]
+
+    def slot(self, column, z):
+        return column * self.p.nz + z
+
+    def sum_of(self, column, z, part):
+        return self.total.at[self.slot(column, z), pl.ds(*part)]
+
+    def add(self, target, *terms):
+        self.store_sum(target, target, *terms)
+
+    def store_sum(self, target, *terms):
+        count = target.shape[0]
+        step = count if count <= 48 else next(s for s in (48, 40, 32, 16) if count % s == 0 and s % 16 == 0)
+
+        def some(i, carry):
+            rs = pl.ds(pl.multiple_of(i * step, 16), step)
+            acc = terms[0][rs, :].astype(F32)
+            for term in terms[1:]:
+                acc = acc + term[rs, :].astype(F32)
+            target[rs, :] = acc.astype(BF16)
+            return carry
+
+        lax.fori_loop(0, count // step, some, 0)
+
+    def send_sib(self, z):
+        p = self.p
+        for column in (3, 1, 2, 0):
+            k = self.slot(column, z)
+            self.w.copy(
+                self.src.at[p.block(column, z, True)], self.side.at[k], self.sib + k, p.sib
+            ).start()
+
+    def take_sib(self, column, z):
+        k = self.slot(column, z)
+        side = self.side.at[k]
+        self.w.copy(side, side, self.sib + k, self.p.sib).wait_recv()
+        own = self.total.at[k] if self.loaded else self.src.at[self.p.block(column, z)]
+        self.store_sum(self.total.at[k], own, side)
+
+    def corner(self, z):
+        p = self.p
+        self.take_sib(3, z)
+        self.w.copy(self.sum_of(3, z, self.first), self.in_first.at[z], self.d1 + z, p.yn).start()
+        self.w.copy(self.sum_of(3, z, self.second), self.in_second.at[z], self.d2 + z, p.xn).start()
+
+    def take_rest(self, z):
+        for column in (1, 2, 0):
+            self.take_sib(column, z)
+
+    def got(self, ref, number):
+        self.w.copy(ref, ref, number, self.p.sib).wait_recv()
+        return ref
+
+    def sides(self, z):
+        p = self.p
+        self.add(self.sum_of(1, z, self.first), self.got(self.in_first.at[z], self.d1 + z))
+        self.w.copy(self.sum_of(1, z, self.early), self.in_x.at[z], self.xs + z, p.xn).start()
+        self.add(self.sum_of(2, z, self.second), self.got(self.in_second.at[z], self.d2 + z))
+        self.w.copy(self.sum_of(2, z, self.early), self.in_y.at[z], self.ys + z, p.yn).start()
+
+    def own(self, z):
+        self.add(
+            self.sum_of(0, z, self.early),
+            self.got(self.in_x.at[z], self.xs + z),
+            self.got(self.in_y.at[z], self.ys + z),
+        )
+        self.along(z, self.sum_of(0, z, self.early), self.in_line, self.line, 0)
+
+    def own_late(self, z):
+        for column in range(4):
+            self.along(z, self.sum_of(column, z, self.late), self.in_late, self.late_line,
+                       column * (self.p.nz + 1))
+
+    def along(self, z, ref, room, number, at):
+        p, nz = self.p, self.p.nz
+        below, above = p.z > 0, p.z < nz - 1
+
+        def take(slot):
+            self.add(ref, self.got(room.at[at + slot], number + at + slot))
+
+        pl.when((z >= p.z) & below)(lambda: take(z))
+        pl.when((z < p.z) & above)(lambda: take(z))
+        pl.when((z == p.z) & above)(lambda: take(nz))
+
+        def send(slot, partner):
+            self.w.copy(ref, room.at[at + slot], number + at + slot, partner).start()
+
+        pl.when(z > p.z)(lambda: send(z, p.me + 8))
+        pl.when(z < p.z)(lambda: send(jnp.where(z == p.z - 1, nz, z), p.me - 8))
+
+    def plane_corner(self):
+        p = self.p
+        self.w.copy(self.sum_of(3, p.z, self.late), self.in_plane.at[0], self.plane, p.yn).start()
+
+    def plane_sides(self):
+        p = self.p
+        self.w.copy(self.sum_of(2, p.z, self.late), self.in_plane.at[2], self.plane + 2, p.yn).start()
+        ref = self.sum_of(1, p.z, self.late)
+        self.add(ref, self.got(self.in_plane.at[0], self.plane))
+        self.w.copy(ref, self.in_plane.at[1], self.plane + 1, p.xn).start()
+
+    def plane_own(self):
+        self.add(
+            self.sum_of(0, self.p.z, self.late),
+            self.got(self.in_plane.at[1], self.plane + 1),
+            self.got(self.in_plane.at[2], self.plane + 2),
+        )
+
+    def steps(self):
+        p, nz = self.p, self.p.nz
+        out = []
+
+        def begin():
+            for d in range(nz - 1, -1, -1):
+                p.level(d, self.send_sib)
+
+        out.append(begin)
+        for t in range(nz + 2):
+            d = nz - 1 - t
+            if d >= 0:
+                out.append(lambda d=d: p.level(d, self.corner))
+            if 0 <= d + 1 < nz:
+                out.append(lambda d=d: p.level(d + 1, self.sides))
+            if d >= 0:
+                out.append(lambda d=d: p.level(d, self.take_rest))
+                out.append(lambda d=d: p.level(d, self.own_late))
+            if d == 0:
+                out.append(self.plane_corner)
+            if d == -1:
+                out.append(self.plane_sides)
+            if 0 <= d + 2 < nz:
+                out.append(lambda d=d: p.level(d + 2, self.own))
+        out.append(self.plane_own)
+        return out
+
+    def drain(self):
+        p, nz = self.p, self.p.nz
+
+        def sent(ref, number):
+            self.w.copy(ref, ref, number, p.sib).wait_send()
+
+        for i in range(3):
+            sent(self.in_plane.at[i], self.plane + i)
+
+        def one(z, carry):
+            for column in range(4):
+                k = self.slot(column, z)
+                sent(self.side.at[k], self.sib + k)
+            sent(self.in_first.at[z], self.d1 + z)
+            sent(self.in_second.at[z], self.d2 + z)
+            sent(self.in_x.at[z], self.xs + z)
+            sent(self.in_y.at[z], self.ys + z)
+
+            def lines(slot):
+                sent(self.in_line.at[slot], self.line + slot)
+                for column in range(4):
+                    at = column * (nz + 1) + slot
+                    sent(self.in_late.at[at], self.late_line + at)
+
+            pl.when(z > p.z)(lambda: lines(z))
+            pl.when(z < p.z)(lambda: lines(jnp.where(z == p.z - 1, nz, z)))
+            return carry
+
+        lax.fori_loop(0, nz, one, 0)
+
+
+def scatter_count(nz):
+    return 4 * nz + 4 * nz + nz + 1 + 4 * (nz + 1) + 3
+
+
+def build_masks(plan, ids_ref, len_ref, key_add, query_one):
+    for r in range(plan.rows):
+        ids = jnp.broadcast_to(ids_ref[r : r + 1, :], (LANES, SLOTS))
+        label = lax.broadcasted_iota(jnp.int32, (LANES, SLOTS), 0)
+        place = lax.broadcasted_iota(jnp.int32, (LANES, SLOTS), 1)
+        start = jnp.sum((ids < label).astype(F32), axis=1, keepdims=True)
+        live = jnp.zeros((LANES, SLOTS), jnp.int32)
+        for j in range(PAIRS):
+            live = jnp.where(label == j, len_ref[r, j, 0] + len_ref[r, j, 1], live)
+        same = ids == label
+        ok = same & (place.astype(F32) - start < live.astype(F32))
+        rs = pl.ds(r * SLOTS, SLOTS)
+        key_add[rs, :] = jnp.where(ok | (label >= PAIRS), 0.0, -1e30).T.astype(BF16)
+        query_one[rs, :] = same.astype(F32).T.astype(BF16)
+
+
+def split_heads(v):
+    lane = lax.broadcasted_iota(jnp.int32, v.shape, 1)
+    zero = jnp.zeros_like(v)
+    return jnp.concatenate(
+        [jnp.where(lane < HEAD_DIM, v, zero), jnp.where(lane < HEAD_DIM, zero, v)], axis=0
+    )
+
+
+def join_heads(v):
+    lane = lax.broadcasted_iota(jnp.int32, (SLOTS, LANES), 1)
+    return jnp.where(lane < HEAD_DIM, v[:SLOTS], v[SLOTS:])
+
+
+def head_pair(i):
+    pairs = HEADS // 2
+    r, p = i // pairs, lax.rem(i, pairs)
+    return (
+        pl.ds(pl.multiple_of(r * SLOTS, 16), SLOTS),
+        pl.ds(pl.multiple_of(p * LANES, LANES), LANES),
+    )
+
+
+def scores_of(rs, cs, qkv, key_add, query_one):
+    q, k, one = qkv[0, rs, cs], qkv[1, rs, cs], query_one[rs, :]
+    q_side = jnp.concatenate([split_heads(q), jnp.concatenate([one, one], axis=0)], axis=1)
+    k_side = jnp.concatenate([k, key_add[rs, :]], axis=1)
+    return dot_nt(k_side, q_side), q, k
+
+
+def attend(i, qkv, key_add, query_one, context, log_totals):
+    rs, cs = head_pair(i)
+    scores, _, _ = scores_of(rs, cs, qkv, key_add, query_one)
+    top = jnp.max(scores, axis=0, keepdims=True)
+    raised = jnp.exp(scores - top)
+    total = jnp.sum(raised, axis=0, keepdims=True)
+    shares = (raised * (1.0 / total)).astype(BF16)
+    log_totals[i] = top + jnp.log(total)
+    context[rs, cs] = join_heads(dot_tn(shares, qkv[2, rs, cs])).astype(BF16)
+
+
+def attend_back(i, qkv, key_add, query_one, log_totals, grad_context, grad_qkv):
+    rs, cs = head_pair(i)
+    scores, q, k = scores_of(rs, cs, qkv, key_add, query_one)
+    shares = jnp.exp(scores - log_totals[i])
+    grad = split_heads(grad_context[rs, cs])
+    grad_shares = dot_nt(qkv[2, rs, cs], grad)
+    inner = jnp.sum(shares * grad_shares, axis=0, keepdims=True)
+    grad_scores = (shares * (grad_shares - inner)).astype(BF16)
+    grad_qkv[2, rs, cs] = dot_nn(shares.astype(BF16), grad).astype(BF16)
+    grad_qkv[1, rs, cs] = dot_nn(grad_scores, split_heads(q)).astype(BF16)
+    grad_qkv[0, rs, cs] = (join_heads(dot_tn(grad_scores, k)) * 0.125).astype(BF16)
+
+
+def run_beside(count, body, steps):
+    def turn(i, carry):
+        body(i)
+        for j, some in enumerate(steps):
+            if some:
+
+                @pl.when(i == j)
+                def _(some=some):
+                    for step in some:
+                        step()
+
+        return carry
+
+    lax.fori_loop(0, count, turn, 0)
+
+
+def deal(steps, count):
+    out = [[] for _ in range(count)]
+    for j, step in enumerate(steps):
+        out[j * count // len(steps)].append(step)
+    return out
+
+
+def joint_weight(plan, ref, b):
+    jr = plan.joint_rows
+    return ref[0 : plan.joint_src, b * jr : (b + 1) * jr, :].reshape(D, D)
+
+
+def out_weight(plan, ref):
+    return ref[plan.joint_src : plan.n].reshape(D, D)
+
+
+def in_weight(plan, ref, c):
+    ir = plan.in_rows
+    return ref[0 : plan.in_src, c * ir : (c + 1) * ir, :].reshape(D, D)
+
+
+def back_weight(plan, ref, c):
+    return ref[back_blocks(plan, c)].reshape(D, D)
+
+
+def back_blocks(plan, c):
+    per = (plan.n - plan.in_src) // 4
+    return pl.ds(plan.in_src + c * per, per)
+
+
+def token_tiles(plan, size, fn):
+    def one(t, carry):
+        fn(pl.ds(pl.multiple_of(t * size, 16), size))
+        return carry
+
+    lax.fori_loop(0, plan.tokens // size, one, 0)
+
+
+def first_kernel(plan, *refs):
+    (x, ids, lens, shard_a, shard_f) = refs[:5]
+    (all_a, all_f, qkv_out, context_out, log_totals, xhat_out, rstd_out, vec) = refs[5:13]
+    (params, qkv, context, xhat, joined_a, joined_f, halo_a, halo_f, end_a, end_f, block_f, vec_own, vec_held,
+     key_add, query_one, send, recv, local) = refs[13:]
+    n, nz = plan.n, plan.nz
+    place = Place(plan)
+    me = place.me
+    wire = Wire(send, recv)
+    tail_a, tail_f = plan.tail_a, plan.tail_f
+    halo_number = 0
+    vec_base = 2
+    bits = n.bit_length() - 1
+    a_base = vec_base + bits
+    f_base = a_base + gather_count(nz)
+
+    end_a[...] = shard_a[plan.unit_a - tail_a : plan.unit_a, :]
+    end_f[...] = shard_f[plan.unit_f - tail_f : plan.unit_f, :]
+    joined_a[tail_a : tail_a + plan.unit_a, :] = shard_a[...]
+    joined_f[tail_f : tail_f + plan.unit_f, :] = shard_f[...]
+    vec_own[0] = jnp.zeros(vec_own.shape[1:], F32)
+    va, vf = 5 * D // LANES, 3 * D // LANES
+
+    @pl.when(me == plan.at_attn_vec[0])
+    def _():
+        vec_own[0, 0:va, :] = shard_a[plan.at_attn_vec[1] : plan.at_attn_vec[1] + va, :]
+        vec_own[0, va + plan.gap : va + plan.gap + vf, :] = shard_f[
+            plan.at_ffn_vec[1] : plan.at_ffn_vec[1] + vf, :
+        ]
+
+    @pl.when(me == plan.at_bias_in[0])
+    def _():
+        vec_own[0, va : va + plan.gap, :] = shard_f[
+            plan.at_bias_in[1] : plan.at_bias_in[1] + plan.gap, :
+        ]
+
+    place.barrier()
+
+    @pl.when(me < n - 1)
+    def _():
+        wire.copy(end_a, halo_a, halo_number, me + 1).start()
+        wire.copy(end_f, halo_f, halo_number + 1, me + 1).start()
+
+    vec_steps = add_over_all(place, wire, vec_base, vec_own, vec_held)
+    vec_steps[0]()
+
+    @pl.when(me > 0)
+    def _():
+        wire.copy(end_a, halo_a, halo_number, me - 1).wait_recv()
+        joined_a[0:tail_a, :] = halo_a[...]
+
+    start = tail_a - plan.shift_a(me)
+    jr = plan.joint_rows
+    mine = params.at[me]
+    cols = [pl.ds(u * LANES, LANES) for u in range(6)]
+
+    @pl.when(me < plan.joint_src)
+    def _():
+        for b in range(3):
+            for u in range(6):
+                mine[b * jr : (b + 1) * jr, cols[u]] = joined_a[
+                    pl.ds(start + 6 * b + u, jr, stride=18), :
+                ].astype(BF16)
+
+    @pl.when(me >= plan.joint_src)
+    def _():
+        for u in range(6):
+            mine[:, cols[u]] = joined_a[pl.ds(start + u, plan.rows_a, stride=6), :].astype(BF16)
+
+    gather_a = Gather(place, wire, a_base, params, plan.rows_a, plan.late_a, plan.half_a)
+    gather_f = Gather(place, wire, f_base, all_f, plan.rows_f, plan.late_f, plan.half_f)
+    steps_a = gather_a.steps()
+    steps_f = gather_f.steps()
+    steps_a[0]()
+
+    @pl.when(me > 0)
+    def _():
+        wire.copy(end_f, halo_f, halo_number + 1, me - 1).wait_recv()
+        joined_f[0:tail_f, :] = halo_f[...]
+
+    start_f = tail_f - plan.shift_f(me)
+    ir = plan.in_rows
+
+    @pl.when(me < plan.in_src)
+    def _():
+        for c in range(4):
+            for u in range(6):
+                block_f[c * ir : (c + 1) * ir, cols[u]] = joined_f[
+                    pl.ds(start_f + 6 * c + u, ir, stride=24), :
+                ].astype(BF16)
+
+    @pl.when(me >= plan.in_src)
+    def _():
+        for u in range(6):
+            block_f[:, cols[u]] = joined_f[pl.ds(start_f + u, plan.rows_f, stride=6), :].astype(BF16)
+
+    own_f = pltpu.make_async_copy(block_f, all_f.at[me], local.at[0])
+    own_f.start()
+
+    def begin_f():
+        own_f.wait()
+        steps_f[0]()
+
+    build_masks(plan, ids, lens, key_add, query_one)
+
+    def finish_vec():
+        whole = vec_own.at[bits]
+        vec[...] = jnp.zeros_like(vec)
+        count = (va + plan.gap + vf) // 6
+        for u in range(6):
+            vec[0:count, cols[u]] = whole[pl.ds(u, count, stride=6), :]
+
+    order = steps_a[1:]
+    at = len(order) - 4
+    order.insert(at, begin_f)
+    for j, step in enumerate(vec_steps[1:] + [finish_vec]):
+        order.insert(2 * j + 1, step)
+    for step in order:
+        step()
+
+    keep_a = pltpu.make_async_copy(params, all_a, local.at[1])
+    keep_a.start()
+    deals = deal(steps_f[1:-1], 3 + HEADS // 2 * plan.rows + 1)
+    for b in range(3):
+        bias = vec[0:1, :] if b == 0 else vec[1:2, :] if b == 2 else None
+        got = dot_nn(x[...], joint_weight(plan, params, b))
+        if bias is not None:
+            got = got + bias
+        got = got.astype(BF16)
+        if b == 0:
+            got = got * jnp.asarray(HEAD_DIM ** (-0.5), BF16)
+        qkv[b] = got
+        for step in deals[b]:
+            step()
+    keep_qkv = pltpu.make_async_copy(qkv, qkv_out, local.at[2])
+    keep_qkv.start()
+    count = HEADS // 2 * plan.rows
+    run_beside(
+        count, lambda i: attend(i, qkv, key_add, query_one, context, log_totals), deals[3 : 3 + count]
+    )
+    keep_context = pltpu.make_async_copy(context, context_out, local.at[3])
+    keep_context.start()
+
+    def norm(rs):
+        v = x[rs, :].astype(F32) + (dot_nn(context[rs, :], out_weight(plan, params)) + vec[2:3, :])
+        centred = v - row_mean(v)
+        rstd = lax.rsqrt(row_mean(centred * centred) + NORM_EPS)
+        xhat[rs, :] = centred * rstd
+        rstd_out[rs, :] = jnp.broadcast_to(rstd, (rstd.shape[0], LANES))
+
+    token_tiles(plan, SLOTS, norm)
+    keep_xhat = pltpu.make_async_copy(xhat, xhat_out, local.at[4])
+    keep_xhat.start()
+    for step in deals[-1] + steps_f[-1:]:
+        step()
+    for copy in (keep_a, keep_qkv, keep_context, keep_xhat):
+        copy.wait()
+    gather_a.drain()
+    gather_f.drain()
+
+    @pl.when(me < n - 1)
+    def _():
+        wire.copy(end_a, halo_a, halo_number, me + 1).wait_send()
+        wire.copy(end_f, halo_f, halo_number + 1, me + 1).wait_send()
+
+
+def vmem_spec():
+    return pl.BlockSpec(memory_space=pltpu.VMEM)
+
+
+def any_spec():
+    return pl.BlockSpec(memory_space=pl.ANY)
+
+
+def first_call(plan, x, ids, lens, shard_a, shard_f):
+    n, t = plan.n, plan.tokens
+    shape = jax.ShapeDtypeStruct
+    turns = HEADS // 2 * plan.rows
+    bits = n.bit_length() - 1
+    units = 80
+    sems = 2 + bits + 2 * gather_count(plan.nz)
+    return pl.pallas_call(
+        functools.partial(first_kernel, plan),
+        name="gather_attend",
+        out_shape=[
+            shape((n, plan.rows_a, D), BF16),
+            shape((n, plan.rows_f, D), BF16),
+            shape((3, t, D), BF16),
+            shape((t, D), BF16),
+            shape((turns, 1, 2 * SLOTS), F32),
+            shape((t, D), F32),
+            shape((t, LANES), F32),
+            shape((16, D), F32),
+        ],
+        in_specs=[vmem_spec(), vmem_spec(), pl.BlockSpec(memory_space=pltpu.SMEM), vmem_spec(), vmem_spec()],
+        out_specs=[
+            any_spec(), any_spec(), any_spec(), any_spec(), vmem_spec(), any_spec(), vmem_spec(), vmem_spec(),
+        ],
+        scratch_shapes=[
+            pltpu.VMEM((n, plan.rows_a, D), BF16),
+            pltpu.VMEM((3, t, D), BF16),
+            pltpu.VMEM((t, D), BF16),
+            pltpu.VMEM((t, D), F32),
+            pltpu.VMEM((plan.tail_a + -(-plan.unit_a // 8) * 8 + 8, LANES), F32),
+            pltpu.VMEM((plan.tail_f + -(-plan.unit_f // 8) * 8 + 8, LANES), F32),
+            pltpu.VMEM((plan.tail_a, LANES), F32),
+            pltpu.VMEM((plan.tail_f, LANES), F32),
+            pltpu.VMEM((plan.tail_a, LANES), F32),
+            pltpu.VMEM((plan.tail_f, LANES), F32),
+            pltpu.VMEM((plan.rows_f, D), BF16),
+            pltpu.VMEM((bits + 1, units, LANES), F32),
+            pltpu.VMEM((bits, units, LANES), F32),
+            pltpu.VMEM((t, LANES), BF16),
+            pltpu.VMEM((t, LANES), BF16),
+            pltpu.SemaphoreType.DMA((sems,)),
+            pltpu.SemaphoreType.DMA((sems,)),
+            pltpu.SemaphoreType.DMA((5,)),
+        ],
+        compiler_params=pltpu.CompilerParams(
+            collective_id=0, has_side_effects=True, vmem_limit_bytes=VMEM_LIMIT
+        ),
+    )(x, ids, lens, shard_a, shard_f)
+
+
+def gelu_with_slope(h):
+    cdf = 0.5 * (1.0 + lax.erf(h * 0.7071067811865476))
+    return h * cdf, cdf + h * jnp.exp(-0.5 * h * h) * 0.3989422804014327
+
+
+def norm_back(grad, xhat, rstd):
+    return rstd * (grad - row_mean(grad) - xhat * row_mean(grad * xhat))
+
+
+def middle_kernel(plan, *refs):
+    (xhat1, rstd1, vec, out_grad, all_f) = refs[:5]
+    (layer_out, grad_first, terms_f, vec_grad) = refs[5:9]
+    (weights, norm_b, active, slope, grad_hidden, acc, grad_ffn, terms, loaded, stored) = refs[9:]
+    per = (plan.n - plan.in_src) // 4
+    ir = plan.in_rows
+
+    def in_part(ref, c):
+        return ref.at[0 : plan.in_src, pl.ds(pl.multiple_of(c * ir, 16), ir), :]
+
+    def back_part(ref, c):
+        return ref.at[pl.ds(plan.in_src + c * per, per)]
+
+    loads = []
+    for c in range(4):
+        loads.append(pltpu.make_async_copy(in_part(all_f, c), in_part(weights, c), loaded.at[2 * c]))
+        loads.append(pltpu.make_async_copy(back_part(all_f, c), back_part(weights, c), loaded.at[2 * c + 1]))
+    for load in loads:
+        load.start()
+    gain_first, shift_first = vec[3:4, :], vec[4:5, :]
+    bias_back, gain_second, shift_second = vec[9:10, :], vec[10:11, :], vec[11:12, :]
+    vec_grad[...] = jnp.zeros_like(vec_grad)
+
+    def enter(rs):
+        v = xhat1[rs, :] * gain_first + shift_first
+        norm_b[rs, :] = v.astype(BF16)
+        acc[rs, :] = v + bias_back
+
+    token_tiles(plan, SLOTS, enter)
+
+    def up(c, carry):
+        pltpu.make_async_copy(in_part(all_f, c), in_part(weights, c), loaded.at[2 * c]).wait()
+        pltpu.make_async_copy(back_part(all_f, c), back_part(weights, c), loaded.at[2 * c + 1]).wait()
+        w_in = in_part(weights, c)[...].reshape(D, D)
+        w_back = back_part(weights, c)[...].reshape(D, D)
+
+        def tile(rs):
+            hidden = dot_nn(norm_b[rs, :], w_in) + vec[pl.ds(5 + c, 1), :]
+            value, incline = gelu_with_slope(hidden)
+            value = value.astype(BF16)
+            active[c, rs, :] = value
+            slope[c, rs, :] = incline.astype(BF16)
+            acc[rs, :] += dot_nn(value, w_back)
+
+        token_tiles(plan, SLOTS, tile)
+        return carry
+
+    lax.fori_loop(0, 4, up, 0)
+
+    def turn(rs):
+        v = acc[rs, :]
+        centred = v - row_mean(v)
+        rstd = lax.rsqrt(row_mean(centred * centred) + NORM_EPS)
+        xhat = centred * rstd
+        layer_out[rs, :] = (xhat * gain_second + shift_second).astype(BF16)
+        cot = out_grad[rs, :].astype(F32)
+        vec_grad[10:11, :] += col_sum(cot * xhat)
+        vec_grad[11:12, :] += col_sum(cot)
+        grad = norm_back(cot * gain_second, xhat, rstd)
+        acc[rs, :] = grad
+        low = grad.astype(BF16)
+        grad_ffn[rs, :] = low
+        vec_grad[9:10, :] += col_sum(low.astype(F32))
+
+    token_tiles(plan, SLOTS, turn)
+
+    def store(part, c, k):
+        return pltpu.make_async_copy(part(terms, c), part(terms_f, c), stored.at[2 * c + k])
+
+    def down(c, carry):
+        back_part(terms, c)[...] = dot_tn(active[c], grad_ffn[...]).astype(BF16).reshape(per, plan.rows_f, D)
+        store(back_part, c, 0).start()
+        w_in = in_part(weights, c)[...].reshape(D, D)
+        w_back = back_part(weights, c)[...].reshape(D, D)
+
+        def tile(rs):
+            grad = (slope[c, rs, :].astype(F32) * dot_nt(grad_ffn[rs, :], w_back)).astype(BF16)
+            grad_hidden[rs, :] = grad
+            vec_grad[pl.ds(5 + c, 1), :] += col_sum(grad.astype(F32))
+            acc[rs, :] += dot_nt(grad, w_in)
+
+        token_tiles(plan, SLOTS, tile)
+        in_part(terms, c)[...] = dot_tn(norm_b[...], grad_hidden[...]).astype(BF16).reshape(plan.in_src, ir, D)
+        store(in_part, c, 1).start()
+        return carry
+
+    lax.fori_loop(0, 4, down, 0)
+
+    def leave(rs):
+        grad, xhat = acc[rs, :], xhat1[rs, :]
+        vec_grad[3:4, :] += col_sum(grad * xhat)
+        vec_grad[4:5, :] += col_sum(grad)
+        grad = norm_back(grad * gain_first, xhat, rstd1[rs, 0:1])
+        grad_first[rs, :] = grad
+        vec_grad[2:3, :] += col_sum(grad.astype(BF16).astype(F32))
+
+    token_tiles(plan, SLOTS, leave)
+    for c in range(4):
+        store(back_part, c, 0).wait()
+        store(in_part, c, 1).wait()
+
+
+def middle_call(plan, xhat, rstd, vec, out_grad, all_f):
+    n, t = plan.n, plan.tokens
+    shape = jax.ShapeDtypeStruct
+    return pl.pallas_call(
+        functools.partial(middle_kernel, plan),
+        name="feed_forward",
+        out_shape=[
+            shape((t, D), BF16), shape((t, D), F32), shape((n, plan.rows_f, D), BF16), shape((16, D), F32),
+        ],
+        in_specs=[vmem_spec(), vmem_spec(), vmem_spec(), vmem_spec(), any_spec()],
+        out_specs=[vmem_spec(), vmem_spec(), any_spec(), vmem_spec()],
+        scratch_shapes=[
+            pltpu.VMEM((n, plan.rows_f, D), BF16),
+            pltpu.VMEM((t, D), BF16),
+            pltpu.VMEM((4, t, D), BF16),
+            pltpu.VMEM((4, t, D), BF16),
+            pltpu.VMEM((t, D), BF16),
+            pltpu.VMEM((t, D), F32),
+            pltpu.VMEM((t, D), BF16),
+            pltpu.VMEM((n, plan.rows_f, D), BF16),
+            pltpu.SemaphoreType.DMA((8,)),
+            pltpu.SemaphoreType.DMA((8,)),
+        ],
+        compiler_params=pltpu.CompilerParams(vmem_limit_bytes=VMEM_LIMIT),
+    )(xhat, rstd, vec, out_grad, all_f)
+
+
+def last_kernel(plan, *refs):
+    (terms_f, all_a, qkv_in, context_in, x_in, grad_first_in, log_totals, ids, lens, vec_grad) = refs[:10]
+    (in_grad, attn_grad, ffn_grad, bias_grad) = refs[10:14]
+    (params, qkv, context, x, grad_first, grad_attn, grad_context, grad_qkv, terms_a, key_add, query_one,
+     vec_own, vec_held, joined_a, joined_f, halo_a, halo_f, send, recv, local, local_f) = refs[14:35]
+    room_f, room_a = refs[35:44], refs[44:53]
+    n, nz = plan.n, plan.nz
+    place = Place(plan)
+    me = place.me
+    wire = Wire(send, recv)
+    bits = n.bit_length() - 1
+    vec_base = 2
+    f_base = vec_base + bits
+    a_base = f_base + scatter_count(nz)
+    total_f, total_a = room_f[0], room_a[0]
+    scatter_f = Scatter(place, wire, f_base, terms_f, plan.rows_f, plan.late_f, plan.half_f, total_f,
+                        room_f[1:], True)
+    scatter_a = Scatter(place, wire, a_base, terms_a, plan.rows_a, plan.late_a, plan.half_a, total_a,
+                        room_a[1:], False)
+
+    pairs = ((all_a, params), (grad_first_in, grad_first), (context_in, context), (qkv_in, qkv), (x_in, x))
+    loads = [pltpu.make_async_copy(a, b, local.at[j]) for j, (a, b) in enumerate(pairs)]
+    own_loads = []
+    for z in range(nz):
+        for column in range(4):
+            k = column * nz + z
+            own_loads.append(
+                pltpu.make_async_copy(terms_f.at[place.block(column, z)], total_f.at[k], local_f.at[k])
+            )
+    for load in loads[:2] + own_loads + loads[2:]:
+        load.start()
+    place.barrier()
+    steps_f = scatter_f.steps()
+    steps_a = scatter_a.steps()
+    steps_f[0]()
+    loads[0].wait()
+    loads[1].wait()
+
+    def low(rs):
+        grad_attn[rs, :] = grad_first[rs, :].astype(BF16)
+        grad_context[rs, :] = dot_nt(grad_attn[rs, :], out_weight(plan, params)).astype(BF16)
+
+    token_tiles(plan, SLOTS, low)
+    loads[2].wait()
+    terms_a[plan.joint_src : n] = (
+        dot_tn(context[...], grad_attn[...]).astype(BF16).reshape(n - plan.joint_src, plan.rows_a, D)
+    )
+    build_masks(plan, ids, lens, key_add, query_one)
+    loads[3].wait()
+    for load in own_loads:
+        load.wait()
+    count = HEADS // 2 * plan.rows
+    run_beside(
+        count,
+        lambda i: attend_back(i, qkv, key_add, query_one, log_totals, grad_context, grad_qkv),
+        deal(steps_f[1:], count),
+    )
+    vec_own[0] = vec_grad[...]
+    vec_own[0, 0:1, :] = col_sum(grad_qkv[0].astype(F32))
+    vec_own[0, 1:2, :] = col_sum(grad_qkv[2].astype(F32))
+    vec_steps = add_over_all(place, wire, vec_base, vec_own, vec_held)
+    vec_steps[0]()
+    loads[4].wait()
+    jr = plan.joint_rows
+    for b in range(3):
+        terms_a[0 : plan.joint_src, b * jr : (b + 1) * jr, :] = (
+            dot_tn(x[...], grad_qkv[b]).astype(BF16).reshape(plan.joint_src, jr, D)
+        )
+    cols = [pl.ds(u * LANES, LANES) for u in range(6)]
+    whole = vec_own.at[bits]
+
+    def lay_f():
+        total = total_f.at[place.z]
+        ir = plan.in_rows
+
+        @pl.when(me < plan.in_src)
+        def _():
+            for c in range(4):
+                for u in range(6):
+                    joined_f[pl.ds(6 * c + u, ir, stride=24), :] = total[
+                        c * ir : (c + 1) * ir, cols[u]
+                    ].astype(F32)
+
+        @pl.when(me >= plan.in_src)
+        def _():
+            for u in range(6):
+                joined_f[pl.ds(u, plan.rows_f, stride=6), :] = total[:, cols[u]].astype(F32)
+
+        @pl.when(me > 0)
+        def _():
+            wire.copy(joined_f.at[0 : plan.tail_f], halo_f, 1, me - 1).start()
+
+    def lay_a():
+        total = total_a.at[place.z]
+
+        @pl.when(me < plan.joint_src)
+        def _():
+            for b in range(3):
+                for u in range(6):
+                    joined_a[pl.ds(6 * b + u, jr, stride=18), :] = total[
+                        b * jr : (b + 1) * jr, cols[u]
+                    ].astype(F32)
+
+        @pl.when(me >= plan.joint_src)
+        def _():
+            for u in range(6):
+                joined_a[pl.ds(u, plan.rows_a, stride=6), :] = total[:, cols[u]].astype(F32)
+
+        @pl.when(me > 0)
+        def _():
+            wire.copy(joined_a.at[0 : plan.tail_a], halo_a, 0, me - 1).start()
+
+    def input_grad(rs):
+        got = grad_first[rs, :]
+        for b in range(3):
+            got = got + dot_nt(grad_qkv[b, rs, :], joint_weight(plan, params, b))
+        in_grad[rs, :] = got
+
+    def join_f():
+        @pl.when(me < n - 1)
+        def _():
+            wire.copy(halo_f, halo_f, 1, me + 1).wait_recv()
+            joined_f[plan.block_f : plan.block_f + plan.tail_f, :] = halo_f[...]
+
+        @pl.when(me == plan.at_bias_in[0])
+        def _():
+            for u in range(6):
+                joined_f[pl.ds(plan.block_f + u, 4, stride=6), :] = whole[5:9, cols[u]]
+            rest = plan.tail_f - plan.gap
+            joined_f[plan.block_f + plan.gap : plan.block_f + plan.tail_f, :] = halo_f[0:rest, :]
+
+        @pl.when(me == n - 1)
+        def _():
+            joined_f[plan.block_f : plan.block_f + plan.tail_f, :] = jnp.zeros((plan.tail_f, LANES), F32)
+            for u in range(6):
+                joined_f[pl.ds(plan.block_f + u, 3, stride=6), :] = whole[9:12, cols[u]]
+
+        ffn_grad[...] = joined_f[pl.ds(plan.shift_f(me), plan.unit_f), :]
+
+    def join_a():
+        @pl.when(me < n - 1)
+        def _():
+            wire.copy(halo_a, halo_a, 0, me + 1).wait_recv()
+            joined_a[plan.block_a : plan.block_a + plan.tail_a, :] = halo_a[...]
+
+        @pl.when(me == n - 1)
+        def _():
+            joined_a[plan.block_a : plan.block_a + plan.tail_a, :] = jnp.zeros((plan.tail_a, LANES), F32)
+            for u in range(6):
+                joined_a[pl.ds(plan.block_a + u, 5, stride=6), :] = whole[0:5, cols[u]]
+
+        attn_grad[...] = joined_a[pl.ds(plan.shift_a(me), plan.unit_a), :]
+
+    steps_a[0]()
+    lay_f()
+    order = steps_a[1:]
+    for j, step in enumerate(vec_steps[1:]):
+        order.insert(2 * j + 1, step)
+    quarter = plan.tokens // 4
+    for j in range(4):
+        order.insert(3 * j + 1, lambda j=j: input_grad(pl.ds(j * quarter, quarter)))
+    for step in order:
+        step()
+    lay_a()
+    join_f()
+    join_a()
+    bias_grad[...] = whole[2:3, :]
+    scatter_f.drain()
+    scatter_a.drain()
+
+    @pl.when(me > 0)
+    def _():
+        wire.copy(halo_f, halo_f, 1, me - 1).wait_send()
+        wire.copy(halo_a, halo_a, 0, me - 1).wait_send()
+
+
+def last_call(plan, terms_f, all_a, qkv, context, x, grad_first, log_totals, ids, lens, vec_grad):
+    n, t, nz = plan.n, plan.tokens, plan.nz
+    shape = jax.ShapeDtypeStruct
+    bits = n.bit_length() - 1
+    sems = 2 + bits + 2 * scatter_count(nz)
+    smem = pl.BlockSpec(memory_space=pltpu.SMEM)
+    return pl.pallas_call(
+        functools.partial(last_kernel, plan),
+        name="attend_back_reduce",
+        out_shape=[
+            shape((t, D), F32), shape((plan.unit_a, LANES), F32), shape((plan.unit_f, LANES), F32),
+            shape((1, D), F32),
+        ],
+        in_specs=[any_spec()] * 6 + [vmem_spec(), vmem_spec(), smem, vmem_spec()],
+        out_specs=[vmem_spec()] * 4,
+        scratch_shapes=[
+            pltpu.VMEM((n, plan.rows_a, D), BF16),
+            pltpu.VMEM((3, t, D), BF16),
+            pltpu.VMEM((t, D), BF16),
+            pltpu.VMEM((t, D), BF16),
+            pltpu.VMEM((t, D), F32),
+            pltpu.VMEM((t, D), BF16),
+            pltpu.VMEM((t, D), BF16),
+            pltpu.VMEM((3, t, D), BF16),
+            pltpu.VMEM((n, plan.rows_a, D), BF16),
+            pltpu.VMEM((t, LANES), BF16),
+            pltpu.VMEM((t, LANES), BF16),
+            pltpu.VMEM((bits + 1, 16, D), F32),
+            pltpu.VMEM((bits, 16, D), F32),
+            pltpu.VMEM((plan.block_a + plan.tail_a + 8, LANES), F32),
+            pltpu.VMEM((plan.block_f + plan.tail_f + 8, LANES), F32),
+            pltpu.VMEM((plan.tail_a, LANES), F32),
+            pltpu.VMEM((plan.tail_f, LANES), F32),
+            pltpu.SemaphoreType.DMA((sems,)),
+            pltpu.SemaphoreType.DMA((sems,)),
+            pltpu.SemaphoreType.DMA((5,)),
+            pltpu.SemaphoreType.DMA((4 * nz,)),
+        ]
+        + Scatter.rooms(nz, plan.rows_f, plan.late_f, plan.half_f)
+        + Scatter.rooms(nz, plan.rows_a, plan.late_a, plan.half_a),
+        compiler_params=pltpu.CompilerParams(
+            collective_id=1, has_side_effects=True, vmem_limit_bytes=VMEM_LIMIT
+        ),
+    )(terms_f, all_a, qkv, context, x, grad_first, log_totals, ids, lens, vec_grad)
+
+
+def fused_body(plan, layer_in, pair_ids, pair_lengths, attn_shard, ffn_shard, out_grad):
+    t = plan.tokens
+    x = layer_in.reshape(t, D)
+    shard_a = attn_shard.astype(F32).reshape(plan.unit_a, LANES)
+    shard_f = ffn_shard.astype(F32).reshape(plan.unit_f, LANES)
+    all_a, all_f, qkv, context, log_totals, xhat, rstd, vec = first_call(
+        plan, x, pair_ids, pair_lengths, shard_a, shard_f
+    )
+    layer_out, grad_first, terms_f, vec_grad = middle_call(
+        plan, xhat, rstd, vec, out_grad.reshape(t, D), all_f
+    )
+    in_grad, attn_grad, ffn_grad, bias_grad = last_call(
+        plan, terms_f, all_a, qkv, context, x, grad_first, log_totals, pair_ids, pair_lengths, vec_grad
+    )
+    return (
+        layer_out.reshape(layer_in.shape),
+        in_grad.reshape(layer_in.shape),
+        attn_grad.reshape(-1),
+        ffn_grad.reshape(-1),
+        bias_grad.reshape(-1),
+    )
 
 
 def unpack_attention(flattened):
@@ -130,7 +1399,7 @@
     return [jnp.moveaxis(piece, 0, 2).reshape(-1, D) for piece in gradients]
 
 
-def body(layer_in, pair_ids, pair_lengths, attn_shard, ffn_shard, out_grad):
+def plain_body(layer_in, pair_ids, pair_lengths, attn_shard, ffn_shard, out_grad):
     row_count = layer_in.shape[0]
     tokens = row_count * SLOTS
     score_scale = HEAD_DIM ** (-0.5)
@@ -248,6 +1517,12 @@
     return (layer_out, in_grad.reshape(row_count, SLOTS, D), attn_grad, ffn_grad, out_bias_grad)
 
 
+def body(layer_in, pair_ids, pair_lengths, attn_shard, ffn_shard, out_grad, devices):
+    plan = Plan(devices, attn_shard.shape[0], ffn_shard.shape[0], layer_in.shape[0])
+    run = functools.partial(fused_body, plan) if plan.fits() else plain_body
+    return run(layer_in, pair_ids, pair_lengths, attn_shard, ffn_shard, out_grad)
+
+
 def solution(mesh):
     placed = (
         P("fsdp", None, None),
@@ -258,7 +1533,7 @@
         P("fsdp", None, None),
     )
     return jax.shard_map(
-        body,
+        functools.partial(body, devices=mesh.shape["fsdp"]),
         mesh=mesh,
         in_specs=placed,
         out_specs=(P("fsdp", None, None), P("fsdp", None, None), P("fsdp"), P("fsdp"), P()),

time: 1190 us -> 235 us (0.20)
  waiting for transfers between devices: 462 us -> 0 us
  other arithmetic: 288 us -> 4.75 us
  local copies, waits for them, and re-layouts: 231 us -> 6.39 us
  Pallas kernels: 0 us -> 222 us
  matrix products: 147 us -> 0 us
  blocking collectives: 41.1 us -> 0 us
  between operations: 14.4 us -> 0.66 us
    unnamed x4 -> x0, waiting for transfers between devices: 384 us -> none
    all_gather x2 -> x0, other arithmetic: 255 us -> none  [the longest x1 153 us: body(): feed_whole = lax.all_gather(ffn_shard, 'fsdp', axis=0, tiled=True)]
    pallas_call x0 -> x3, Pallas kernels: none -> 222 us  [the longest x1 99.8 us: last_call(): pl.pallas_call(functools.partial(last_kernel, plan), name='attend_back_re...]
    dot_general x33 -> x0, matrix products: 147 us -> none  [the longest x4 32.3 us: contract_cols(): lax.dot_general(one_side, other_side, (((1,), (1,)), ((), ())), preferred...]
    unnamed x102 -> x8, local copies, waits for them, and re-layouts: 88.3 us -> 6.39 us
    all_gather x2 -> x0, waiting for transfers between devices: 78 us -> none  [the longest x1 78 us: body(): att_whole = lax.all_gather(attn_shard, 'fsdp', axis=0, tiled=True)]
    reshape x12 -> x0, local copies, waits for them, and re-layouts: 72.5 us -> none  [the longest x1 14.8 us: body(): projected = projected.reshape(row_count, SLOTS, 3, HEADS, HEAD_DIM)]
    psum x1 -> x0, blocking collectives: 41.1 us -> none  [body(): out_bias_grad = lax.psum(grad_bias_out, 'fsdp')]
  transfers between devices with their start and end apart: 3 -> 0, of which waited for: 2 -> 0; matrix products, arithmetic and copies ran while one was open for 18% -> 0% of each run, Pallas kernels for 0% -> 0%
where the time goes in v1:
time: 235 us; the launch traced here: 234 us
  Pallas kernels  222 us (94%)
  local copies, waits for them, and re-layouts  6.39 us (3%)
  other arithmetic  4.75 us (2%)
    pallas_call x1, Pallas kernels, last_call(): pl.pallas_call(functools.partial(last_kernel, plan), name='attend_back_re...  99.8 us
    pallas_call x1, Pallas kernels, first_call(): pl.pallas_call(functools.partial(first_kernel, plan), name='gather_attend...  77.5 us
    pallas_call x1, Pallas kernels, middle_call(): pl.pallas_call(functools.partial(middle_kernel, plan), name='feed_forward...  45.2 us
    unnamed x8, local copies, waits for them, and re-layouts  6.39 us

profile of v1, /device:TPU:1, one launch (start us, length us, event | category | flops | bytes accessed | tf_op | source)
XLA Modules:
  0.0 234.3 jit_solution(4440595565256337031)
XLA Ops:
  0.6 1.4 copy.11.refs_2_.refs_8_
  2.0 1.6 bitcast_convert_fusion.1.refs_3_
  3.6 1.8 bitcast_convert_fusion.refs_4_
  5.5 77.5 %gather_attend.1 = (bf16[32,96,768]{2,1,0:T(8,128)(2,1)}, bf16[32,192,768]{2,1,0:T(8,128)(2,1)}, bf16[3,832,768]{2,1,0:T(8,128)(2,1)}, bf16[832,768]{1,0:T(8,128...) custom-call(bf16[832,768]{1,0:T(8,128)(2,1)} %bitcast.12, ...), custom_call_target="tpu_custom_call" | custom-call | tf_op jit(solution)/shard_map/gather_attend/pallas_call | solution.py:860
  83.0 45.2 %feed_forward.1 = (bf16[832,768]{1,0:T(8,128)(2,1)}, f32[832,768]{1,0:T(8,128)}, bf16[32,192,768]{2,1,0:T(8,128)(2,1)}, f32[16,768]{1,0:T(8,128)}) custom-call(f32[832,768]{1,0:T(8,128)} %get-tuple-element.21.refs_0_, f32[832,128]{1,0:T(8,128)} %get-tuple-element.22.refs_1_, f32[16,768]{1,0:T(8,128)} %get-tuple-element.23.refs_2_, ...), custom_call_target="tpu_custom_call" | custom-call | tf_op jit(solution)/shard_map/feed_forward/pallas_call | solution.py:1017
  128.2 99.8 %attend_back_reduce.1 = (f32[832,768]{1,0:T(8,128)}, f32[577,128]{1,0:T(8,128)}, f32[1154,128]{1,0:T(8,128)}, f32[1,768]{1,0:T(1,128)}) custom-call(bf16[32,192,768]{2,1,0:T(8,128)(2,1)} %get-tuple-element.26.refs_0_, bf16[32,96,768]{2,1,0:T(8,128)(2,1)} %get-tuple-element.27.refs_1_, bf16[3,832,768]{2,1,0:T(8,128)(2,1)} %get-tuple-element.28.refs_2_, ...), custom_call_target="tpu_custom_call" | custom-call | tf_op jit(solution)/shard_map/attend_back_reduce/pallas_call | solution.py:1223
  227.9 1.3 reduce
  229.2 0.0 copy-start.1
  229.2 0.0 copy-start
  229.2 3.4 %copy.16 = f32[2,416,768]{2,1,0:T(8,128)} copy(f32[2,416,768]{2,1,0:T(8,128)} %bitcast.14) | data formatting | bytes 5111808
  232.7 0.0 copy-done.1
  232.7 0.7 copy.17
  233.4 0.0 copy-done
  233.4 0.9 copy.18
Async XLA Ops:
  229.2 3.4 %copy-start.1 = (f32[577,128]{1,0:T(8,128)S(1)}, f32[577,128]{1,0:T(8,128)}, u32[]{:S(2)}) copy-start(f32[577,128]{1,0:T(8,128)} %get-tuple-element.34) | copy-start | bytes 886276
  229.2 4.2 %copy-start = (f32[1154,128]{1,0:T(8,128)S(1)}, f32[1154,128]{1,0:T(8,128)}, u32[]{:S(2)}) copy-start(f32[1154,128]{1,0:T(8,128)} %get-tuple-element.35) | copy-start | bytes 1772548
